TPU v7x, 32 devices: a whole 2x2x4 slice. The times are simulated.
32 devices in a mesh: row: 8 (over z, y), col: 4 (over x, core).
Axes of the slice: x: 2, y: 2, z: 4, core: 2. Of those that a mesh axis runs over, the one named last changes fastest.
Arguments:
- a_blocks: float32 [128, 8, 125, 125], P('row', 'col'), may hold values from -0.1875 to 0.1875
- a_pattern: int32 [128, 8], P('row', 'col'), may hold values 0 or 1
- row_owner: int32 [128], replicated, may hold values from 0 to 127, as said below
- prolong: float32 [8, 24, 125, 125], P('row', 'col'), may hold values from -6 to 6
- p_pattern: int32 [8, 24], P('row', 'col'), may hold values 0 or 1
- prolong_slab: float32 [128, 8, 125, 125], P('row'), may hold values from -0.0625 to 0.0625
Outputs:
- coarse: float32 [8, 24, 125, 125], P('row', 'col')
Inputs may be any that keep to these rules, and one draw needn't show every extreme that they name: row_owner is a permutation; the 16 element-order rows e with e // 16 equal go to at most 2 positions p of any one value p // 16, and exactly 2 for each value they reach.
All inputs are finite; a program needn't handle non-finite values. No bound on the sum of `a_pattern` or of `p_pattern` on one device may be relied on, other than what follows from the above.
Results may differ from a plain program's by a relative error of at most 0.0001.
Values sent between devices are 32-bit elements; how exact they have to be, the bound alone decides.
A program may use at most 128 MiB of HBM per device.

v0:
```python
import jax
import jax.numpy as jnp
from jax import lax
from jax.sharding import PartitionSpec as P

CAP = 2


def ranks_of(targets):
    width = targets.shape[-1]
    same = targets[..., :, None] == targets[..., None, :]
    lower = jnp.arange(width)[:, None] > jnp.arange(width)[None, :]
    return jnp.sum(jnp.where(same & lower, 1, 0), axis=-1).astype(jnp.int32)


def pick(rows, at):
    return jnp.stack([lax.dynamic_index_in_dim(rows, at[i], 0, keepdims=False) for i in range(at.shape[0])])


def shards(a_blocks, a_pattern, row_owner, prolong, p_pattern, prolong_slab):
    width = a_blocks.shape[0]
    count = lax.axis_size("row")
    me = lax.axis_index("row")
    masked = a_blocks * a_pattern.astype(jnp.float32)[:, :, None, None]
    p_masked = prolong * p_pattern.astype(jnp.float32)[:, :, None, None]
    p_full = lax.all_gather(p_masked, "row", axis=0, tiled=True)

    table = row_owner.reshape(count, width)
    ranks = ranks_of(table // width)
    targets = lax.dynamic_index_in_dim(table, me, 0, keepdims=False) // width
    mine = lax.dynamic_index_in_dim(ranks, me, 0, keepdims=False)
    slot = targets * CAP + mine
    hit = slot[None, :] == jnp.arange(count * CAP, dtype=jnp.int32)[:, None]
    order = jnp.sum(jnp.where(hit, jnp.arange(width, dtype=jnp.int32)[None, :], 0), axis=1)
    packed = pick(masked, order)
    packed = packed.reshape((count, CAP) + masked.shape[1:])
    received = lax.all_to_all(packed, "row", split_axis=0, concat_axis=0, tiled=True)
    received = received.reshape((count * CAP,) + masked.shape[1:])
    wanted = table[None] == (me * width + jnp.arange(width, dtype=jnp.int32))[:, None, None]
    source = jnp.arange(count, dtype=jnp.int32)[:, None] * CAP + ranks
    where = jnp.sum(jnp.where(wanted, source[None], 0), axis=(1, 2))
    grid_a = pick(received, where)
    part = jnp.einsum(
        "maxy,mkxz->akyz",
        prolong_slab,
        grid_a,
        precision=lax.Precision.HIGH,
        preferred_element_type=jnp.float32,
    )
    mine = lax.psum_scatter(part, "row", scatter_dimension=0, tiled=True)
    mid = lax.all_gather(mine, "col", axis=1, tiled=True)
    return jnp.einsum(
        "akyx,knxz->anyz",
        mid,
        p_full,
        precision=lax.Precision.HIGH,
        preferred_element_type=jnp.float32,
    )


def solution(mesh):
    in_specs = (
        P("row", "col", None, None),
        P("row", "col"),
        P(),
        P("row", "col", None, None),
        P("row", "col"),
        P("row", None, None, None),
    )
    out_specs = P("row", "col", None, None)
    return jax.shard_map(shards, mesh=mesh, in_specs=in_specs, out_specs=out_specs, check_vma=False)
```

profile of v0, /device:TPU:13, one launch (start us, length us, event | category | flops | bytes accessed | tf_op | source)
XLA Modules:
  0.0 266.0 jit_solution(4542487792375120371)
XLA Ops:
  6.5 0.7 reshape.110
  7.3 0.3 select_reduce_fusion.1
  7.6 0.1 select_reduce_fusion.2
  7.7 0.7 fusion.16
  28.4 0.7 convert_element_type.7
  29.0 0.1 copy.30
  29.8 2.3 broadcast_multiply_fusion
  32.1 0.7 dynamic-slice_dynamic-update-slice_fusion.31
  33.4 0.7 dynamic-slice_dynamic-update-slice_fusion.30
  34.6 0.7 dynamic-slice_dynamic-update-slice_fusion.29
  35.9 0.7 dynamic-slice_dynamic-update-slice_fusion.28
  37.2 0.7 dynamic-slice_dynamic-update-slice_fusion.27
  38.5 0.7 dynamic-slice_dynamic-update-slice_fusion.26
  39.8 0.7 dynamic-slice_dynamic-update-slice_fusion.25
  41.2 0.7 dynamic-slice_dynamic-update-slice_fusion.24
  42.4 0.7 dynamic-slice_dynamic-update-slice_fusion.23
  43.8 0.7 dynamic-slice_dynamic-update-slice_fusion.22
  45.0 0.7 dynamic-slice_dynamic-update-slice_fusion.21
  46.3 0.7 dynamic-slice_dynamic-update-slice_fusion.20
  47.6 0.7 dynamic-slice_dynamic-update-slice_fusion.19
  48.9 0.7 dynamic-slice_dynamic-update-slice_fusion.18
  50.2 0.7 dynamic-slice_dynamic-update-slice_fusion.17
  51.5 0.7 dynamic-slice_dynamic-update-slice_fusion.16
  52.2 5.7 %all-to-all-start = ((f32[8,2,2,125,125]{4,2,3,1,0:T(2,128)}), f32[8,2,2,125,125]{4,2,3,1,0:T(2,128)}, u32[]{:S(2)}, u32[]{:S(2)}) async-start(f32[8,2,2,125,125]{4,2,3,1,0:T(2,128)} %bitcast.84), calls=%async_computation | async-start | bytes 4096000 | tf_op jit(solution)/shard_map/all_to_all | solution.py:37
  57.8 0.0 all-reduce.3.cloned.1.call-start
  57.8 0.1 broadcast_add_fusion
  57.9 0.4 select_reduce_fusion
  58.4 0.7 fusion.15
  88.7 13.8 %all-to-all-done = f32[8,2,2,125,125]{4,2,3,1,0:T(2,128)} async-done(((f32[8,2,2,125,125]{4,2,3,1,0:T(2,128)}), f32[8,2,2,125,125]{4,2,3,1,0:T(2,128)}, u32[]{:S(2)}, u32[]{:S(2)}) %all-to-all-start) | async-done | bytes 2000032 | tf_op jit(solution)/shard_map/all_to_all | solution.py:37
  102.5 2.8 %copy.31 = f32[8,2,2,125,125]{3,4,1,0,2:T(8,128)S(1)} copy(f32[8,2,2,125,125]{4,2,3,1,0:T(2,128)} %all-to-all-done) | data formatting | bytes 4000000 | tf_op jit(solution)/shard_map/all_to_all | solution.py:37
  105.8 8.5 %fusion.4 = f32[8,2,125,125]{2,3,0,1:T(8,128)S(1)} fusion(f32[16,8,125,125]{3,1,2,0:T(8,128)} %param.11, f32[16,2,125,125]{2,3,0,1:T(8,128)S(1)} %dynamic-slice_dynamic-update-slice_fusion), kind=kOutput, calls=%fused_computation.4 | convolution fusion | flops 3000000000 | bytes 11000000 | tf_op jit(solution)/shard_map/maxy,mkxz->akyz/dot_general | solution.py:43
  114.2 0.0 copy-start
  114.3 0.0 copy-start.1
  114.3 0.0 copy-start.2
  114.3 1.4 copy.33
  115.7 0.0 all-reduce.3.cloned.1.call-update
  115.7 0.0 all-gather.2.cloned.1.call-start
  115.8 0.4 copy.29
  116.1 0.8 broadcast_multiply_fusion.1
  117.0 0.0 all-gather.2.cloned.1.call-update
  117.0 0.6 dynamic-slice
  117.6 76.1 %all-reduce.3.cloned.1.call-done = f32[8,2,125,125]{3,1,2,0:T(2,128)} async-done(((f32[8,2,125,125]{3,1,2,0:T(2,128)}), f32[8,2,125,125]{3,1,2,0:T(2,128)}) %all-reduce.3.cloned.1.call-update) | async-done | bytes 1000016
  193.7 1.6 constant_dynamic-slice_fusion.2
  195.3 0.1 copy.34
  195.4 8.4 %all_gather.7 = f32[1,8,125,125]{3,0,2,1:T(1,128)S(1)} all-gather(f32[1,2,125,125]{3,0,2,1:T(1,128)S(1)} %copy.34), channel_id=1, replica_groups=mesh['row'=8,'col'=4] {'col'}, dimensions={1}, use_global_device_ids=true | all-gather | bytes 625000 | tf_op jit(solution)/shard_map/all_gather | solution.py:51
  203.8 51.0 %all-gather.2.cloned.1.call-done = f32[8,6,125,125]{2,3,0,1:T(8,128)} async-done(((f32[1,6,125,125]{2,3,0,1:T(8,128)}), f32[8,6,125,125]{2,3,0,1:T(8,128)}) %all-gather.2.cloned.1.call-update) | async-done | bytes 3000016 | tf_op jit(solution)/shard_map/all_gather | solution.py:26
  254.8 3.3 %convolution_bitcast_fusion = f32[1,6,125,125]{2,3,1,0:T(8,128)S(1)} fusion(f32[8,6,125,125]{2,3,0,1:T(8,128)} %all-gather.2.cloned.1.call-done, f32[1,8,125,125]{3,0,2,1:T(1,128)S(1)} %all_gather.7), kind=kOutput, calls=%fused_computation.5 | convolution fusion | flops 562499968 | bytes 3875000 | tf_op jit(solution)/shard_map/akyx,knxz->anyz/dot_general | solution.py:52
  258.1 1.0 copy.37
  (25 shorter events, 0.4 us)
Async XLA Ops:
  52.2 50.3 %all-to-all-start = ((f32[8,2,2,125,125]{4,2,3,1,0:T(2,128)}), f32[8,2,2,125,125]{4,2,3,1,0:T(2,128)}, u32[]{:S(2)}, u32[]{:S(2)}) async-start(f32[8,2,2,125,125]{4,2,3,1,0:T(2,128)} %bitcast.84), calls=%async_computation | async-start | bytes 4096000 | tf_op jit(solution)/shard_map/all_to_all | solution.py:37
  57.8 135.9 %all-reduce.3.cloned.1.call-start = ((), (), s32[]{:S(2)}) async-start(), calls=%async_computation.2 | async-start | bytes 2048000
  114.2 1.5 copy-start
  114.3 1.9 copy-start.1
  114.3 2.7 %copy-start.2 = (u32[32]{0:T(128)S(1)}, u32[32]{0:T(128)}, u32[]{:S(2)}) copy-start(u32[32]{0:T(128)} %constant.116) | copy-start | bytes 388
  115.7 139.1 %all-gather.2.cloned.1.call-start = ((), (), s32[]{:S(2)}) async-start(), calls=%async_computation.1 | async-start | bytes 3538944 | tf_op jit(solution)/shard_map/all_gather | solution.py:26
Sparse Core Ops, SparseCore 0:
  115.8 77.8 all-reduce.2
  195.9 58.8 all-gather.1
where the time goes:
time: 271 us; the launch traced here: 266 us
  waiting for transfers between devices  141 us (52%)
  between operations  73.3 us (27%)
  local copies, waits for them, and re-layouts  21.1 us (8%)
  matrix products  11.8 us (4%)
  blocking collectives  8.39 us (3%)
  starting transfers between devices  5.71 us (2%)
  other arithmetic  4.83 us (2%)
    unnamed x3, waiting for transfers between devices  76.1 us
    all_gather x1, waiting for transfers between devices, shards(): p_full = lax.all_gather(p_masked, 'row', axis=0, tiled=True)  51 us
    all_to_all x1, waiting for transfers between devices, shards(): lax.all_to_all(packed, 'row', split_axis=0, concat_axis=0, tiled=True)  13.8 us
    unnamed x39, local copies, waits for them, and re-layouts  12.8 us
    dot_general x1, matrix products, shards(): jnp.einsum('maxy,mkxz->akyz', prolong_slab, grid_a, precision=lax.Precisi...  8.49 us
    all_gather x1, blocking collectives, shards(): mid = lax.all_gather(mine, 'col', axis=1, tiled=True)  8.39 us
    all_to_all x1, starting transfers between devices, shards(): lax.all_to_all(packed, 'row', split_axis=0, concat_axis=0, tiled=True)  5.66 us
  transfers between devices with their start and end apart: 3, of which 3 were waited for; matrix products, arithmetic and copies ran while one was open for 2% of the time, Pallas kernels for 0%

commit v1 on v0

v1 whole, which is shorter than its diff:
```python
import functools

import jax
import jax.numpy as jnp
from jax import lax
from jax.experimental import pallas as pl
from jax.experimental.pallas import tpu as pltpu
from jax.sharding import PartitionSpec as P

CAP = 2
Z = 4
L = 128
MESH = pl.DeviceIdType.MESH


def split(v):
    hi = v.astype(jnp.bfloat16)
    lo = (v - hi.astype(jnp.float32)).astype(jnp.bfloat16)
    return hi, lo


def mul3(ah, al, bh, bl):
    dot = functools.partial(jnp.dot, preferred_element_type=jnp.float32)
    return dot(ah, bh) + (dot(ah, bl) + dot(al, bh))


def kernel(
    R, C, a_hbm, s_hbm, p_in, owner, a_pat, p_pat, out,
    a_v, s_v, asend, arecv, stage, sh, sl, ath, atl, macc, mrecv, mfull, mth, mtl, pbuf, ph, plo, total,
    load, a_s, a_r, m_s, m_r, g_s, g_r, u_s, u_r, d_s, d_r, y_s, y_r,
):
    W, KP, B = a_v.shape[0], a_v.shape[1], a_v.shape[2]
    NA, NJ = s_v.shape[1], p_in.shape[1]
    Y = R // Z
    me, col = lax.axis_index("row"), lax.axis_index("col")
    z, y = lax.div(me, Y), lax.rem(me, Y)

    load_a = pltpu.make_async_copy(a_hbm, a_v, load.at[0])
    load_s = pltpu.make_async_copy(s_hbm, s_v, load.at[1])
    load_a.start()
    load_s.start()

    barrier = pltpu.get_barrier_semaphore()
    for i in range(1, R):
        pl.semaphore_signal(barrier, inc=1, device_id={"row": lax.rem(me + i, R)}, device_id_type=MESH)
    for i in range(1, C):
        pl.semaphore_signal(barrier, inc=1, device_id={"col": lax.rem(col + i, C)}, device_id_type=MESH)

    for n in range(NJ):
        pbuf[me, n] = jnp.zeros((L, L), jnp.float32)
        pbuf[me, n, 0:B, 0:B] = p_in[0, n] * p_pat[0, n].astype(jnp.float32)

    pl.semaphore_wait(barrier, R + C - 2)

    def p_copy(slot, target, s_sem, r_sem):
        return pltpu.make_async_remote_copy(
            src_ref=pbuf.at[slot], dst_ref=pbuf.at[slot], send_sem=s_sem, recv_sem=r_sem,
            device_id={"row": target}, device_id_type=MESH,
        )

    def up(t):
        return p_copy((z - t) * Y + y, me + Y, u_s.at[t], u_r.at[t + 1])

    def down(t):
        return p_copy((z + t) * Y + y, me - Y, d_s.at[t], d_r.at[t + 1])

    def across(zo, i):
        return p_copy(zo * Y + y, z * Y + lax.rem(y + i, Y), y_s.at[zo * Y + i], y_r.at[zo * Y + i])

    def hop(t):
        @pl.when(z >= t)
        def _():
            if t > 0:
                p_copy((z - t) * Y + y, me, u_s.at[t], u_r.at[t]).wait_recv()

            @pl.when(z < Z - 1)
            def _():
                up(t).start()

            for i in range(1, Y):
                across(z - t, i).start()

        @pl.when(z + t < Z)
        def _():
            if t > 0:
                p_copy((z + t) * Y + y, me, d_s.at[t], d_r.at[t]).wait_recv()

            @pl.when(z > 0)
            def _():
                down(t).start()

            if t > 0:
                for i in range(1, Y):
                    across(z + t, i).start()

    hop(0)

    def pair(source, target):
        first, last = jnp.int32(W), jnp.int32(-1)
        for e in range(W):
            hit = lax.div(owner[source * W + e], W) == target
            first = jnp.minimum(first, jnp.where(hit, e, W))
            last = jnp.maximum(last, jnp.where(hit, e, -1))
        valid = last >= 0
        return (jnp.where(valid, first, 0), jnp.where(valid, last, 0)), valid

    def a_copy(step):
        return pltpu.make_async_remote_copy(
            src_ref=asend.at[step], dst_ref=arecv.at[step], send_sem=a_s.at[step], recv_sem=a_r.at[step],
            device_id={"row": lax.rem(me + step, R)}, device_id_type=MESH,
        )

    def pack(buf, step):
        rows, valid = pair(me, lax.rem(me + step, R))
        for s in range(CAP):
            for k in range(KP):
                scale = jnp.where(valid, a_pat[rows[s], k], 0).astype(jnp.float32)
                buf[step, s, k] = jnp.zeros((L, L), jnp.float32)
                buf[step, s, k, 0:B, 0:B] = a_v[rows[s], k] * scale

    def step_of(j):
        half = lax.div(j + 1, 2)
        return R // 2 + half * (1 - 2 * lax.rem(j, 2))

    load_a.wait()

    def send_step(j, carry):
        step = step_of(j)
        pack(asend, step)
        a_copy(step).start()
        return carry

    lax.fori_loop(0, R - 1, send_step, 0)
    pack(arecv, 0)
    stage[...] = jnp.zeros_like(stage)
    macc[...] = jnp.zeros_like(macc)
    load_s.wait()

    def work(step, arrives):
        source = lax.rem(me - step + R, R)
        rows, valid = pair(source, me)
        for s in range(CAP):
            g = jnp.where(valid, owner[source * W + rows[s]] - me * W, 0)

            def slab(b, carry):
                for h in range(2):
                    stage[2 * b + h, 0:B, 0:B] = s_v[g, 2 * b + h]
                for h in range(2):
                    hi, lo = split(stage[2 * b + h])
                    sh[b, s * L : (s + 1) * L, h * L : (h + 1) * L] = hi
                    sl[b, s * L : (s + 1) * L, h * L : (h + 1) * L] = lo
                return carry

            lax.fori_loop(0, NA // 2, slab, 0)
        if arrives:
            a_copy(step).wait_recv()
        for s in range(CAP):
            for k in range(KP):
                hi, lo = split(arecv[step, s, k].T)
                ath[k * L : (k + 1) * L, s * L : (s + 1) * L] = hi
                atl[k * L : (k + 1) * L, s * L : (s + 1) * L] = lo

        def add(b, carry):
            r = mul3(ath[...], atl[...], sh[b], sl[b])
            macc[2 * b] += r[:, 0:L]
            macc[2 * b + 1] += r[:, L : 2 * L]
            return carry

        lax.fori_loop(0, NA // 2, add, 0)

    def remote_step(j, carry):
        work(step_of(j), True)
        return carry

    work(0, False)
    at = 0
    for t in range(1, Z):
        hop(t)
        until = (R - 1) * t // Z if t < Z - 1 else R - 1
        lax.fori_loop(at, until, remote_step, 0)
        at = until

    def m_copy(step):
        target = lax.rem(me + step, R)
        return pltpu.make_async_remote_copy(
            src_ref=macc.at[target], dst_ref=mrecv.at[step], send_sem=m_s.at[step], recv_sem=m_r.at[step],
            device_id={"row": target}, device_id_type=MESH,
        )

    def m_send(j, carry):
        m_copy(step_of(j)).start()
        return carry

    lax.fori_loop(0, R - 1, m_send, 0)

    for zo in range(Z):
        for i in range(1, Y):
            across(zo, i).wait_recv()

    def p_split(r, carry):
        for n in range(NJ):
            hi, lo = split(pbuf[r, n])
            at = pl.ds(pl.multiple_of(r * L, L), L)
            ph[at, n * L : (n + 1) * L] = hi
            plo[at, n * L : (n + 1) * L] = lo
        return carry

    lax.fori_loop(0, R, p_split, 0)

    mfull[col] = macc[me]

    def m_add(j, carry):
        step = step_of(j)
        m_copy(step).wait_recv()
        mfull[col] += mrecv[step]
        return carry

    lax.fori_loop(0, R - 1, m_add, 0)

    def g_copy(i):
        return pltpu.make_async_remote_copy(
            src_ref=mfull.at[col], dst_ref=mfull.at[col], send_sem=g_s.at[i], recv_sem=g_r.at[i],
            device_id={"col": lax.rem(col + i, C)}, device_id_type=MESH,
        )

    for i in range(1, C):
        g_copy(i).start()
    total[...] = jnp.zeros_like(total)

    for i in range(C):
        source = lax.rem(col - i + C, C)
        if i > 0:
            g_copy(i).wait_recv()
        for k in range(KP):
            hi, lo = split(mfull[source, k * L : (k + 1) * L, :].T)
            mth[:, k * L : (k + 1) * L] = hi
            mtl[:, k * L : (k + 1) * L] = lo
        rows = pl.ds(pl.multiple_of(source * KP * L, KP * L), KP * L)
        total[...] += mul3(mth[...], mtl[...], ph[rows, :], plo[rows, :])

    for n in range(NJ):
        out[0, n] = total[0:B, n * L : n * L + B]

    def a_done(j, carry):
        a_copy(j + 1).wait_send()
        m_copy(j + 1).wait_send()
        return carry

    lax.fori_loop(0, R - 1, a_done, 0)
    for i in range(1, C):
        g_copy(i).wait_send()
    for t in range(Z):
        @pl.when((z >= t) & (z < Z - 1))
        def _():
            up(t).wait_send()

        @pl.when((z + t < Z) & (z > 0))
        def _():
            down(t).wait_send()

    for zo in range(Z):
        for i in range(1, Y):
            across(zo, i).wait_send()


def shards(a_blocks, a_pattern, row_owner, prolong, p_pattern, prolong_slab):
    R, C = lax.axis_size("row"), lax.axis_size("col")
    W, KP, B = a_blocks.shape[:3]
    NA, NJ = prolong_slab.shape[1], prolong.shape[1]
    f32, bf16 = jnp.float32, jnp.bfloat16
    dma = pltpu.SemaphoreType.DMA
    vmem = pl.BlockSpec(memory_space=pltpu.VMEM)
    smem = pl.BlockSpec(memory_space=pltpu.SMEM)
    hbm = pl.BlockSpec(memory_space=pl.ANY)
    return pl.pallas_call(
        functools.partial(kernel, R, C),
        out_shape=jax.ShapeDtypeStruct((1, NJ, B, B), f32),
        in_specs=[hbm, hbm, vmem, smem, smem, smem],
        out_specs=vmem,
        scratch_shapes=[
            pltpu.VMEM((W, KP, B, B), f32),
            pltpu.VMEM((W, NA, B, B), f32),
            pltpu.VMEM((R, CAP, KP, L, L), f32),
            pltpu.VMEM((R, CAP, KP, L, L), f32),
            pltpu.VMEM((NA, L, L), f32),
            pltpu.VMEM((NA // 2, CAP * L, 2 * L), bf16),
            pltpu.VMEM((NA // 2, CAP * L, 2 * L), bf16),
            pltpu.VMEM((KP * L, CAP * L), bf16),
            pltpu.VMEM((KP * L, CAP * L), bf16),
            pltpu.VMEM((NA, KP * L, L), f32),
            pltpu.VMEM((R, KP * L, L), f32),
            pltpu.VMEM((C, KP * L, L), f32),
            pltpu.VMEM((L, KP * L), bf16),
            pltpu.VMEM((L, KP * L), bf16),
            pltpu.VMEM((R, NJ, L, L), f32),
            pltpu.VMEM((R * L, NJ * L), bf16),
            pltpu.VMEM((R * L, NJ * L), bf16),
            pltpu.VMEM((L, NJ * L), f32),
            dma((2,)),
            dma((R,)), dma((R,)), dma((R,)), dma((R,)), dma((C,)), dma((C,)),
            dma((Z,)), dma((Z + 1,)), dma((Z,)), dma((Z + 1,)), dma((R,)), dma((R,)),
        ],
        compiler_params=pltpu.CompilerParams(
            collective_id=0, has_side_effects=True, vmem_limit_bytes=58 * 1024 * 1024
        ),
    )(a_blocks, prolong_slab, prolong, row_owner, a_pattern, p_pattern)


def solution(mesh):
    in_specs = (
        P("row", "col", None, None),
        P("row", "col"),
        P(),
        P("row", "col", None, None),
        P("row", "col"),
        P("row", None, None, None),
    )
    out_specs = P("row", "col", None, None)
    return jax.shard_map(shards, mesh=mesh, in_specs=in_specs, out_specs=out_specs, check_vma=False)
```

time: 271 us -> 127 us (0.47); the launches traced: 266 us -> 125 us
  waiting for transfers between devices: 141 us -> 0 us
  Pallas kernels: 0 us -> 109 us
  between operations: 73.3 us -> 0.01 us
  matrix products: 11.8 us -> 0 us
  blocking collectives: 8.39 us -> 0 us
  starting transfers between devices: 5.71 us -> 0 us
  other arithmetic: 4.83 us -> 0 us
  local copies, waits for them, and re-layouts: 21.1 us -> 16.5 us
    pallas_call x0 -> x1, Pallas kernels: none -> 109 us  [shards(): pl.pallas_call(functools.partial(kernel, R, C), out_shape=jax.ShapeDtypeS...]
    unnamed x3 -> x0, waiting for transfers between devices: 76.1 us -> none
    all_gather x1 -> x0, waiting for transfers between devices: 51 us -> none  [shards(): p_full = lax.all_gather(p_masked, 'row', axis=0, tiled=True)]
    all_to_all x1 -> x0, waiting for transfers between devices: 13.8 us -> none  [shards(): lax.all_to_all(packed, 'row', split_axis=0, concat_axis=0, tiled=True)]
    dot_general x2 -> x0, matrix products: 11.8 us -> none  [the longest x1 8.49 us: shards(): jnp.einsum('maxy,mkxz->akyz', prolong_slab, grid_a, precision=lax.Precisi...]
    all_gather x1 -> x0, blocking collectives: 8.39 us -> none  [shards(): mid = lax.all_gather(mine, 'col', axis=1, tiled=True)]
    all_to_all x1 -> x0, starting transfers between devices: 5.66 us -> none  [shards(): lax.all_to_all(packed, 'row', split_axis=0, concat_axis=0, tiled=True)]
    mul x4 -> x0, other arithmetic: 3.18 us -> none  [the longest x1 2.34 us: shards(): masked = a_blocks * a_pattern.astype(jnp.float32)[:, :, None, None]]
  transfers between devices with their start and end apart: 3 -> 0, of which waited for: 3 -> 0; matrix products, arithmetic and copies ran while one was open for 2% -> 0% of each run, Pallas kernels for 0% -> 0%
where the time goes in v1:
time: 127 us; the launch traced here: 125 us
  Pallas kernels  109 us (86%)
  local copies, waits for them, and re-layouts  16.5 us (13%)
    pallas_call x1, Pallas kernels, shards(): pl.pallas_call(functools.partial(kernel, R, C), out_shape=jax.ShapeDtypeS...  109 us
    unnamed x4, local copies, waits for them, and re-layouts  14.4 us

profile of v1, /device:TPU:13, one launch (start us, length us, event | category | flops | bytes accessed | tf_op | source)
XLA Modules:
  0.0 125.3 jit_solution(3273310893938190708)
XLA Ops:
  0.0 1.4 %copy.10.a_pat = s32[16,2]{1,0:T(8,128)} copy(s32[16,2]{0,1:T(2,128)} %param.7) | data formatting | bytes 256 | tf_op args[1]
  1.4 1.8 %copy.9.p_in = f32[1,6,125,125]{3,2,1,0:T(8,128)} copy(f32[1,6,125,125]{3,0,2,1:T(1,128)} %param.9) | data formatting | bytes 750000 | tf_op args[3]
  3.1 3.2 %copy.7.a_hbm = f32[16,2,125,125]{3,2,1,0:T(8,128)} copy(f32[16,2,125,125]{3,1,2,0:T(2,128)} %param.6) | data formatting | bytes 4000000 | tf_op args[0]
  6.4 8.0 %copy.8.s_hbm = f32[16,8,125,125]{3,2,1,0:T(8,128)} copy(f32[16,8,125,125]{3,1,2,0:T(8,128)} %param.11) | data formatting | bytes 16000000 | tf_op args[5]
  14.4 108.7 %shard_map.64 = f32[1,6,125,125]{3,2,1,0:T(8,128)} custom-call(f32[16,2,125,125]{3,2,1,0:T(8,128)} %copy.7.a_hbm, f32[16,8,125,125]{3,2,1,0:T(8,128)} %copy.8.s_hbm, f32[1,6,125,125]{3,2,1,0:T(8,128)} %copy.9.p_in, s32[128]{0:T(128)} %owner.1, s32[16,2]{1,0:T(8,128)} %copy.10.a_pat, s32[1,6]{1,0:T(1,128)} %p_pat.1), custom_call_target="tpu_custom_call" | custom-call | tf_op jit(solution)/shard_map/pallas_call | solution.py:275
  123.1 2.1 %copy.11 = f32[1,6,125,125]{3,0,2,1:T(1,128)} copy(f32[1,6,125,125]{3,2,1,0:T(8,128)} %shard_map.64) | data formatting | bytes 750000 | tf_op jit(solution)/shard_map/pallas_call | solution.py:275

commit v2 on v1

--- a/solution.py
+++ b/solution.py
@@ -30,7 +30,7 @@
     load, a_s, a_r, m_s, m_r, g_s, g_r, u_s, u_r, d_s, d_r, y_s, y_r,
 ):
     W, KP, B = a_v.shape[0], a_v.shape[1], a_v.shape[2]
-    NA, NJ = s_v.shape[1], p_in.shape[1]
+    NA, NJ = s_v.shape[1] // B, p_in.shape[1]
     Y = R // Z
     me, col = lax.axis_index("row"), lax.axis_index("col")
     z, y = lax.div(me, Y), lax.rem(me, Y)
@@ -114,7 +114,7 @@
         rows, valid = pair(me, lax.rem(me + step, R))
         for s in range(CAP):
             for k in range(KP):
-                scale = jnp.where(valid, a_pat[rows[s], k], 0).astype(jnp.float32)
+                scale = jnp.where(valid, a_pat[k, rows[s]], 0).astype(jnp.float32)
                 buf[step, s, k] = jnp.zeros((L, L), jnp.float32)
                 buf[step, s, k, 0:B, 0:B] = a_v[rows[s], k] * scale
 
@@ -144,7 +144,7 @@
 
             def slab(b, carry):
                 for h in range(2):
-                    stage[2 * b + h, 0:B, 0:B] = s_v[g, 2 * b + h]
+                    stage[2 * b + h, 0:B, 0:B] = s_v[g, pl.ds(2 * b + h, B, stride=NA), :]
                 for h in range(2):
                     hi, lo = split(stage[2 * b + h])
                     sh[b, s * L : (s + 1) * L, h * L : (h + 1) * L] = hi
@@ -268,6 +268,7 @@
     W, KP, B = a_blocks.shape[:3]
     NA, NJ = prolong_slab.shape[1], prolong.shape[1]
     f32, bf16 = jnp.float32, jnp.bfloat16
+    slab = prolong_slab.transpose(0, 2, 1, 3).reshape(W, B * NA, B)
     dma = pltpu.SemaphoreType.DMA
     vmem = pl.BlockSpec(memory_space=pltpu.VMEM)
     smem = pl.BlockSpec(memory_space=pltpu.SMEM)
@@ -279,7 +280,7 @@
         out_specs=vmem,
         scratch_shapes=[
             pltpu.VMEM((W, KP, B, B), f32),
-            pltpu.VMEM((W, NA, B, B), f32),
+            pltpu.VMEM((W, B * NA, B), f32),
             pltpu.VMEM((R, CAP, KP, L, L), f32),
             pltpu.VMEM((R, CAP, KP, L, L), f32),
             pltpu.VMEM((NA, L, L), f32),
@@ -303,7 +304,7 @@
         compiler_params=pltpu.CompilerParams(
             collective_id=0, has_side_effects=True, vmem_limit_bytes=58 * 1024 * 1024
         ),
-    )(a_blocks, prolong_slab, prolong, row_owner, a_pattern, p_pattern)
+    )(a_blocks, slab, prolong, row_owner, a_pattern.T, p_pattern)
 
 
 def solution(mesh):

time: 127 us -> 119 us (0.937)
  local copies, waits for them, and re-layouts: 16.5 us -> 7.11 us
    unnamed x4 -> x2, local copies, waits for them, and re-layouts: 14.4 us -> 4.98 us
where the time goes in v2:
time: 119 us; the launch traced here: 117 us
  Pallas kernels  109 us (92%)
  local copies, waits for them, and re-layouts  7.11 us (6%)
    pallas_call x1, Pallas kernels, shards(): pl.pallas_call(functools.partial(kernel, R, C), out_shape=jax.ShapeDtypeS...  109 us
    unnamed x2, local copies, waits for them, and re-layouts  4.98 us

profile of v2, /device:TPU:13, one launch (start us, length us, event | category | flops | bytes accessed | tf_op | source)
XLA Modules:
  0.0 116.6 jit_solution(7473224196897382119)
XLA Ops:
  0.0 1.8 %copy.8.p_in = f32[1,6,125,125]{3,2,1,0:T(8,128)} copy(f32[1,6,125,125]{3,0,2,1:T(1,128)} %param.9) | data formatting | bytes 750000 | tf_op args[3]
  1.8 3.2 %copy.7.a_hbm = f32[16,2,125,125]{3,2,1,0:T(8,128)} copy(f32[16,2,125,125]{3,1,2,0:T(2,128)} %param.6) | data formatting | bytes 4000000 | tf_op args[0]
  5.0 109.5 %shard_map.64 = f32[1,6,125,125]{3,2,1,0:T(8,128)} custom-call(f32[16,2,125,125]{3,2,1,0:T(8,128)} %copy.7.a_hbm, f32[16,1000,125]{2,1,0:T(8,128)} %bitcast.4, f32[1,6,125,125]{3,2,1,0:T(8,128)} %copy.8.p_in, s32[128]{0:T(128)} %owner.1, s32[2,16]{1,0:T(2,128)} %bitcast.5, s32[1,6]{1,0:T(1,128)} %p_pat.1), custom_call_target="tpu_custom_call" | custom-call | tf_op jit(solution)/shard_map/pallas_call | solution.py:276
  114.5 2.1 %copy.9 = f32[1,6,125,125]{3,0,2,1:T(1,128)} copy(f32[1,6,125,125]{3,2,1,0:T(8,128)} %shard_map.64) | data formatting | bytes 750000 | tf_op jit(solution)/shard_map/pallas_call | solution.py:276

commit v3 on v2

--- a/solution.py
+++ b/solution.py
@@ -30,7 +30,7 @@
     load, a_s, a_r, m_s, m_r, g_s, g_r, u_s, u_r, d_s, d_r, y_s, y_r,
 ):
     W, KP, B = a_v.shape[0], a_v.shape[1], a_v.shape[2]
-    NA, NJ = s_v.shape[1] // B, p_in.shape[1]
+    NA, NJ = s_v.shape[1] // B, p_in.shape[0]
     Y = R // Z
     me, col = lax.axis_index("row"), lax.axis_index("col")
     z, y = lax.div(me, Y), lax.rem(me, Y)
@@ -46,10 +46,6 @@
     for i in range(1, C):
         pl.semaphore_signal(barrier, inc=1, device_id={"col": lax.rem(col + i, C)}, device_id_type=MESH)
 
-    for n in range(NJ):
-        pbuf[me, n] = jnp.zeros((L, L), jnp.float32)
-        pbuf[me, n, 0:B, 0:B] = p_in[0, n] * p_pat[0, n].astype(jnp.float32)
-
     pl.semaphore_wait(barrier, R + C - 2)
 
     def p_copy(slot, target, s_sem, r_sem):
@@ -93,7 +89,6 @@
                 for i in range(1, Y):
                     across(z + t, i).start()
 
-    hop(0)
 
     def pair(source, target):
         first, last = jnp.int32(W), jnp.int32(-1)
@@ -131,12 +126,23 @@
         return carry
 
     lax.fori_loop(0, R - 1, send_step, 0)
+    for n in range(NJ):
+        pbuf[me, n] = jnp.zeros((L, L), jnp.float32)
+        pbuf[me, n, 0:B, 0:B] = p_in[n, :, 0, :] * p_pat[0, n].astype(jnp.float32)
+    hop(0)
     pack(arecv, 0)
     stage[...] = jnp.zeros_like(stage)
     macc[...] = jnp.zeros_like(macc)
     load_s.wait()
 
-    def work(step, arrives):
+    def m_copy(step):
+        target = lax.rem(me + step, R)
+        return pltpu.make_async_remote_copy(
+            src_ref=macc.at[target], dst_ref=mrecv.at[step], send_sem=m_s.at[step], recv_sem=m_r.at[step],
+            device_id={"row": target}, device_id_type=MESH,
+        )
+
+    def work(step, arrives, last=False):
         source = lax.rem(me - step + R, R)
         rows, valid = pair(source, me)
         for s in range(CAP):
@@ -160,10 +166,15 @@
                 ath[k * L : (k + 1) * L, s * L : (s + 1) * L] = hi
                 atl[k * L : (k + 1) * L, s * L : (s + 1) * L] = lo
 
-        def add(b, carry):
+        def add(i, carry):
+            b = lax.rem(i + lax.div(me, 2), NA // 2)
             r = mul3(ath[...], atl[...], sh[b], sl[b])
             macc[2 * b] += r[:, 0:L]
             macc[2 * b + 1] += r[:, L : 2 * L]
+            for h in range(2 if last else 0):
+                @pl.when(2 * b + h != me)
+                def _():
+                    m_copy(lax.rem(2 * b + h - me + R, R)).start()
             return carry
 
         lax.fori_loop(0, NA // 2, add, 0)
@@ -176,22 +187,10 @@
     at = 0
     for t in range(1, Z):
         hop(t)
-        until = (R - 1) * t // Z if t < Z - 1 else R - 1
+        until = (R - 1) * t // Z if t < Z - 1 else R - 2
         lax.fori_loop(at, until, remote_step, 0)
         at = until
-
-    def m_copy(step):
-        target = lax.rem(me + step, R)
-        return pltpu.make_async_remote_copy(
-            src_ref=macc.at[target], dst_ref=mrecv.at[step], send_sem=m_s.at[step], recv_sem=m_r.at[step],
-            device_id={"row": target}, device_id_type=MESH,
-        )
-
-    def m_send(j, carry):
-        m_copy(step_of(j)).start()
-        return carry
-
-    lax.fori_loop(0, R - 1, m_send, 0)
+    work(step_of(jnp.int32(R - 2)), True, last=True)
 
     for zo in range(Z):
         for i in range(1, Y):
@@ -304,7 +303,7 @@
         compiler_params=pltpu.CompilerParams(
             collective_id=0, has_side_effects=True, vmem_limit_bytes=58 * 1024 * 1024
         ),
-    )(a_blocks, slab, prolong, row_owner, a_pattern.T, p_pattern)
+    )(a_blocks, slab, prolong.transpose(1, 2, 0, 3), row_owner, a_pattern.T, p_pattern)
 
 
 def solution(mesh):

time: 119 us -> 115 us (0.966); the launches traced: 117 us -> 115 us
  local copies, waits for them, and re-layouts: 7.11 us -> 5.33 us
    unnamed x2 -> x1, local copies, waits for them, and re-layouts: 4.98 us -> 3.2 us
where the time goes in v3:
time: 115 us
  Pallas kernels  110 us (96%)
  local copies, waits for them, and re-layouts  5.33 us (5%)
    pallas_call x1, Pallas kernels, shards(): pl.pallas_call(functools.partial(kernel, R, C), out_shape=jax.ShapeDtypeS...  110 us
    unnamed x1, local copies, waits for them, and re-layouts  3.2 us

profile of v3, /device:TPU:13, one launch (start us, length us, event | category | flops | bytes accessed | tf_op | source)
XLA Modules:
  0.0 114.9 jit_solution(11708208031197909699)
XLA Ops:
  0.0 3.2 %copy.7.a_hbm = f32[16,2,125,125]{3,2,1,0:T(8,128)} copy(f32[16,2,125,125]{3,1,2,0:T(2,128)} %param.6) | data formatting | bytes 4000000 | tf_op args[0]
  3.2 109.6 %shard_map.64 = f32[1,6,125,125]{3,2,1,0:T(8,128)} custom-call(f32[16,2,125,125]{3,2,1,0:T(8,128)} %copy.7.a_hbm, f32[16,1000,125]{2,1,0:T(8,128)} %bitcast.5, f32[6,125,1,125]{3,2,1,0:T(1,128)} %bitcast.6, s32[128]{0:T(128)} %owner.1, s32[2,16]{1,0:T(2,128)} %bitcast.7, s32[1,6]{1,0:T(1,128)} %p_pat.1), custom_call_target="tpu_custom_call" | custom-call | tf_op jit(solution)/shard_map/pallas_call | solution.py:275
  112.8 2.1 %copy.8 = f32[1,6,125,125]{3,0,2,1:T(1,128)} copy(f32[1,6,125,125]{3,2,1,0:T(8,128)} %shard_map.64) | data formatting | bytes 750000 | tf_op jit(solution)/shard_map/pallas_call | solution.py:275
